TPU v7x, 32 devices: a whole 2x2x4 slice. The times are simulated.
32 devices in a mesh: parts: 2 (over y), track: 4 (over z), tm: 2 (over x), coef: 2 (over core).
Axes of the slice: x: 2, y: 2, z: 4, core: 2. Of those that a mesh axis runs over, the one named last changes fastest.
Arguments:
- sector_ids: int32 [12288], P(('parts', 'track', 'tm')), parts along dimension 0, may hold values from 0 to 63, as said below
- observed: float32 [3, 12288], P(None, ('parts', 'track', 'tm')), parts along dimension 1, may hold values from -6 to 6
- weights: float32 [3, 12288], P(None, ('parts', 'track', 'tm')), parts along dimension 1, may hold values from 0.3 to 3
- coefficients: float32 [2048, 128], P(('parts', 'track')), parts along dimension 0, may hold values from -6 to 6
- tile_index: int32 [128, 12], P(('parts', 'track', 'tm'), 'coef'), parts along dimension 0, may hold values from 0 to 1023, as said below
- tile_count: int32 [128], P(('parts', 'track', 'tm')), parts along dimension 0, may hold values from 3 to 12
- sensitivity: bfloat16 [128, 12, 3, 128, 128], P(('parts', 'track', 'tm'), 'coef'), parts along dimension 0, may hold values from -0.15625 to 0.15625
Outputs:
- gradient: float32 [2048, 128], P(('parts', 'track')), parts along dimension 0
There are 2 independent parts, one for each index of `parts`. A program takes and returns all parts, laid end to end along the dimension named above; each array names one. Nothing has to cross between parts.
Inputs may be any that keep to these rules, and one draw needn't show every extreme that they name: `sector_ids`: the rows of one index of track and tm fall in at most 192 rows into the 8 consecutive sectors of any one index, and some pair reaches 192; the sectors of each index receive exactly 768 rows in all; each sector holds at most 128 rows, and every index holds a sector with exactly 128. `tile_index`: entries at positions from tile_count on are arbitrary blocks and take no part. Block n belongs to track index n // 256. Of the 48 entries held by one index of track, tm and coef (its sectors' rows, its coef share of the columns), live or not, at most 24 name blocks of any one track index, and every such device has a track index named exactly 24 times.
All inputs are finite; a program needn't handle non-finite values.
Results may differ from a plain program's by a relative error of at most 0.0037.
Values may be sent and summed in bfloat16 or wider, within the bound.
A program may use at most 64 MiB of HBM per device.

v0:
```python
import jax
import jax.numpy as jnp
from jax import lax
from jax.sharding import PartitionSpec as P

HUBER = 2.0


def per_device(sector_ids, observed, weights, coefficients, tile_index, tile_count, sensitivity):
    sector_total = tile_index.shape[0]
    half_k = tile_index.shape[1]
    slot_count = sensitivity.shape[3]
    block_width = sensitivity.shape[4]
    owners = lax.axis_size(("track", "tm"))
    row_total = sector_ids.shape[0]
    capacity = 2 * row_total // owners
    rounded = coefficients.astype(jnp.bfloat16)
    every_block = lax.all_gather(rounded, "track", axis=0, tiled=True)
    owner_of = sector_ids // sector_total
    local_sector = sector_ids % sector_total
    onehot = (owner_of[:, None] == jnp.arange(owners, dtype=jnp.int32)[None, :]).astype(jnp.int32)
    ranking = jnp.sum((jnp.cumsum(onehot, axis=0) - 1) * onehot, axis=1)
    placing = owner_of * capacity + ranking
    payload = jnp.concatenate([observed, weights], axis=0)
    outgoing = jnp.zeros((6, owners * capacity), jnp.float32).at[:, placing].set(payload)
    outgoing = jnp.transpose(outgoing.reshape(6, owners, capacity), (1, 0, 2))
    labels = jnp.full((owners * capacity,), -1, jnp.int32).at[placing].set(local_sector)
    labels = labels.reshape(owners, capacity)
    got_rows, got_labels = (
        lax.all_to_all(outgoing, ("track", "tm"), split_axis=0, concat_axis=0, tiled=True),
        lax.all_to_all(labels, ("track", "tm"), split_axis=0, concat_axis=0, tiled=True),
    )
    received = jnp.transpose(got_rows, (1, 0, 2)).reshape(6, owners * capacity)
    flat_labels = got_labels.reshape(owners * capacity)
    member = (flat_labels[:, None] == jnp.arange(sector_total, dtype=jnp.int32)[None, :]).astype(
        jnp.int32
    )
    within = jnp.sum((jnp.cumsum(member, axis=0) - 1) * member, axis=1)
    target = jnp.where(
        flat_labels >= 0, flat_labels * slot_count + within, sector_total * slot_count
    )
    gridded = jnp.zeros((6, sector_total * slot_count + 1), jnp.float32).at[:, target].set(received)
    gridded = jnp.transpose(gridded[:, :-1].reshape(6, sector_total, slot_count), (1, 0, 2))
    observed_tiles = gridded[:, :3]
    weight_tiles = gridded[:, 3:]
    k_global = lax.axis_index("coef") * half_k + jnp.arange(half_k, dtype=jnp.int32)
    active = k_global[None, :] < tile_count[:, None]
    blocks = jnp.take(every_block, tile_index, axis=0)
    blocks = jnp.where(active[:, :, None], blocks, jnp.zeros_like(blocks))
    partial_pred = jnp.einsum(
        "skcjb,skb->scj", sensitivity, blocks, preferred_element_type=jnp.float32
    )
    predicted = lax.psum(partial_pred, "coef")
    scaled = weight_tiles * (predicted - observed_tiles)
    force = (weight_tiles * scaled / jnp.sqrt(1.0 + (scaled / HUBER) ** 2)).astype(jnp.bfloat16)
    tile_grad = jnp.einsum("skcjb,scj->skb", sensitivity, force, preferred_element_type=jnp.float32)
    tile_grad = jnp.where(active[:, :, None], tile_grad, jnp.zeros_like(tile_grad))
    block_total = every_block.shape[0]
    partial_grad = jnp.zeros((block_total, block_width), jnp.float32)
    partial_grad = partial_grad.at[tile_index.reshape(-1)].add(tile_grad.reshape(-1, block_width))
    summed = lax.psum_scatter(partial_grad, "track", scatter_dimension=0, tiled=True)
    gradient = lax.psum(summed, ("tm", "coef"))
    return gradient


def solution(mesh):
    placed = (
        P(("parts", "track", "tm")),
        P(None, ("parts", "track", "tm")),
        P(None, ("parts", "track", "tm")),
        P(("parts", "track"), None),
        P(("parts", "track", "tm"), "coef"),
        P(("parts", "track", "tm")),
        P(("parts", "track", "tm"), "coef", None, None, None),
    )
    return jax.shard_map(
        per_device,
        mesh=mesh,
        in_specs=placed,
        out_specs=P(("parts", "track"), None),
        check_vma=False,
    )
```

profile of v0, /device:TPU:0, one launch (start us, length us, event | category | flops | bytes accessed | tf_op | source)
XLA Modules:
  0.0 135.0 jit_solution(9949122944024813271)
XLA Ops:
  6.5 0.7 add_select_fusion
  7.2 1.7 %reduce-window.14 = s32[8,6,128]{2,0,1:T(8,128)S(1)} reduce-window(s32[8,6,128]{2,0,1:T(8,128)S(1)} %fusion.13, s32[]{:T(128)} %constant.40.clone.1), window={size=1x1x128 pad=0_0x0_0x127_0}, to_apply=%region_0.1 | reduce-window | flops 780288 | bytes 49156 | tf_op jit(solution)/shard_map/reduce-window
  8.9 0.1 slice.30
  9.0 0.1 copy.24
  9.2 0.2 reduce-window.15
  9.3 0.1 copy.25
  9.4 0.1 fusion.11
  9.5 3.4 %scatter_custom_fusion = s32[1536]{0:T(1024)S(1)} fusion(s32[768]{0:T(1024)S(1)} %compare_select_fusion.2, s32[768]{0:T(1024)S(1)} %get-tuple-element.7, s32[]{:T(128)} %constant.74.clone.1), kind=kCustom, calls=%fused_computation.50 | custom fusion | bytes 6148 | tf_op jit(solution)/shard_map/scatter | solution.py:27
  12.9 0.7 all_to_all.9
  13.6 7.3 %all-to-all-start = ((s32[8,1,192]{2,1,0:T(1,128)}), s32[8,1,192]{2,1,0:T(1,128)S(1)}, u32[]{:S(2)}, u32[]{:S(2)}) async-start(s32[8,1,192]{2,1,0:T(1,128)} %all_to_all.9), calls=%async_computation | async-start | bytes 16384 | tf_op jit(solution)/shard_map/all_to_all | solution.py:31
  20.8 0.7 compare_select_fusion.1
  21.5 0.8 reshape.166
  22.3 0.7 maximum_bitcast_fusion
  23.0 0.2 copy.26
  23.2 4.4 %scatter_custom_fusion.1 = f32[6,1536]{0,1:T(8,128)S(1)} fusion(s32[768]{0:T(1024)S(1)} %compare_select_fusion.2, f32[768,6]{1,0:T(8,128)S(1)} %copy.26, f32[]{:T(128)} %constant.39.clone.1), kind=kCustom, calls=%fused_computation.7 | custom fusion | bytes 36868 | tf_op jit(solution)/shard_map/scatter | solution.py:25
  27.6 1.0 copy.27
  28.6 0.9 convert_element_type.18
  29.5 14.5 %all_gather.3 = bf16[1024,128]{1,0:T(8,128)(2,1)S(1)} all-gather(bf16[256,128]{1,0:T(8,128)(2,1)S(1)} %convert_element_type.18), channel_id=1, replica_groups=mesh['parts'=2,'track'=4,'tm'=2,'coef'=2] {'track'}, dimensions={0}, use_global_device_ids=true | all-gather | bytes 327680 | tf_op jit(solution)/shard_map/all_gather | solution.py:18
  44.0 0.1 reshape.175
  44.0 0.6 gather_fusion
  44.7 0.8 compare_and_fusion
  45.4 0.1 select_bitcast_fusion
  45.5 3.7 %fusion = f32[8,1,3,128,1]{3,1,4,2,0:T(1,128)S(1)} fusion(bf16[8,6,3,128,128]{4,3,2,1,0:T(8,128)(2,1)} %param.13, bf16[8,6,128,1,1]{2,1,0,3,4:T(8,128)(2,1)S(1)} %select_bitcast_fusion), kind=kOutput, calls=%fused_computation.5 | convolution fusion | flops 4718592 | bytes 4743168 | tf_op jit(solution)/shard_map/skcjb,skb->scj/dot_general | solution.py:50
  49.2 3.3 %psum.14 = f32[8,3,128]{2,0,1:T(8,128)S(1)} all-reduce(f32[8,3,128]{2,0,1:T(8,128)S(1)} %bitcast.50), channel_id=1, replica_groups=mesh['parts'=2,'track'=4,'tm'=2,'coef'=2] {'coef'}, use_global_device_ids=true, to_apply=%region_9.10 | all-reduce | flops 3072 | bytes 24576 | tf_op jit(solution)/shard_map/psum | solution.py:53
  52.5 0.0 all-to-all-done
  52.5 5.7 %all-to-all-start.1 = ((f32[8,6,192]{2,1,0:T(8,128)}), f32[8,6,192]{2,1,0:T(8,128)S(1)}, u32[]{:S(2)}, u32[]{:S(2)}) async-start(f32[8,6,192]{2,1,0:T(8,128)} %bitcast.8), calls=%async_computation.1 | async-start | bytes 131072 | tf_op jit(solution)/shard_map/all_to_all | solution.py:30
  58.2 0.0 reduce-scatter.2.cloned.1.call-start
  58.3 0.1 eq.61
  58.4 0.1 eq.57
  58.5 2.3 %reduce-window.16 = s32[8,12,128]{2,1,0:T(8,128)S(1)} reduce-window(s32[8,12,128]{2,1,0:T(8,128)S(1)} %fusion.8, s32[]{:T(128)} %constant.40.clone.1), window={size=1x1x128 pad=0_0x0_0x127_0}, to_apply=%region_4.5 | reduce-window | flops 1560576 | bytes 98308 | tf_op jit(solution)/shard_map/reduce-window.2
  60.7 0.3 slice_reduce_fusion
  61.0 0.2 reduce-window.19
  61.2 0.1 add_bitcast_fusion
  61.3 0.1 mul.43
  61.4 0.1 ge.21
  61.6 3.5 %all-to-all-done.1 = f32[8,6,192]{2,1,0:T(8,128)S(1)} async-done(((f32[8,6,192]{2,1,0:T(8,128)}), f32[8,6,192]{2,1,0:T(8,128)S(1)}, u32[]{:S(2)}, u32[]{:S(2)}) %all-to-all-start.1) | async-done | bytes 36896 | tf_op jit(solution)/shard_map/all_to_all | solution.py:30
  65.1 0.1 reshape.198
  65.2 0.3 copy.29
  65.5 4.4 %scatter_custom_fusion.2 = f32[6,1025]{0,1:T(8,128)S(1)} fusion(s32[1536]{0:T(1024)S(1)} %fusion.17, f32[1536,6]{1,0:T(8,128)S(1)} %copy.29, f32[]{:T(128)} %constant.39.clone.1), kind=kCustom, calls=%fused_computation.9 | custom fusion | bytes 24604 | tf_op jit(solution)/shard_map/scatter | solution.py:42
  70.0 0.2 copy.36
  70.2 3.1 %fusion.15 = f32[8,1,6,128,1]{3,1,4,2,0:T(1,128)S(1)} fusion(bf16[8,6,3,128,128]{4,3,2,1,0:T(8,128)(2,1)} %param.13, bf16[8,3,128,1,1]{2,0,1,3,4:T(8,128)(2,1)S(1)} %fusion.18), kind=kOutput, calls=%fused_computation.34 | convolution fusion | flops 4718592 | bytes 4749312 | tf_op jit(solution)/shard_map/skcjb,scj->skb/dot_general | solution.py:56
  73.3 0.1 bitcast_select_fusion
  73.4 1.5 %scatter_custom_fusion.3 = f32[1024,128]{1,0:T(8,128)} fusion(s32[48]{0:T(128)S(1)} %fusion.23, f32[48,128]{1,0:T(8,128)S(1)} %reshape.209, f32[]{:T(128)} %constant.39.clone.1), kind=kCustom, calls=%fused_computation.11 | custom fusion | flops 6144 | bytes 524292 | tf_op jit(solution)/shard_map/scatter-add | solution.py:60
  74.9 0.0 reduce-scatter.2.cloned.1.call-update
  75.0 0.0 all-reduce.2.cloned.1.call-start
  75.0 19.6 %reduce-scatter.2.cloned.1.call-done = f32[256,128]{1,0:T(8,128)} async-done(((f32[1024,128]{1,0:T(8,128)}), f32[256,128]{1,0:T(8,128)}) %reduce-scatter.2.cloned.1.call-update) | async-done | bytes 131088 | tf_op jit(solution)/shard_map/reduce_scatter | solution.py:61
  94.6 0.0 all-reduce.2.cloned.1.call-update
  94.7 32.0 %all-reduce.2.cloned.1.call-done = f32[256,128]{1,0:T(8,128)} async-done(((f32[256,128]{1,0:T(8,128)}), f32[256,128]{1,0:T(8,128)}) %all-reduce.2.cloned.1.call-update) | async-done | bytes 131088 | tf_op jit(solution)/shard_map/psum | solution.py:62
  126.6 1.6 %copy.49 = f32[256,128]{1,0:T(8,128)} copy(f32[256,128]{1,0:T(8,128)} %all-reduce.2.cloned.1.call-done) | data formatting | bytes 262144
  (16 shorter events, 0.3 us)
Async XLA Ops:
  13.6 38.9 %all-to-all-start = ((s32[8,1,192]{2,1,0:T(1,128)}), s32[8,1,192]{2,1,0:T(1,128)S(1)}, u32[]{:S(2)}, u32[]{:S(2)}) async-start(s32[8,1,192]{2,1,0:T(1,128)} %all_to_all.9), calls=%async_computation | async-start | bytes 16384 | tf_op jit(solution)/shard_map/all_to_all | solution.py:31
  52.5 12.6 %all-to-all-start.1 = ((f32[8,6,192]{2,1,0:T(8,128)}), f32[8,6,192]{2,1,0:T(8,128)S(1)}, u32[]{:S(2)}, u32[]{:S(2)}) async-start(f32[8,6,192]{2,1,0:T(8,128)} %bitcast.8), calls=%async_computation.1 | async-start | bytes 131072 | tf_op jit(solution)/shard_map/all_to_all | solution.py:30
  58.2 36.4 %reduce-scatter.2.cloned.1.call-start = ((), (), s32[]{:S(2)}) async-start(), calls=%async_computation.3 | async-start | bytes 655360 | tf_op jit(solution)/shard_map/reduce_scatter | solution.py:61
  75.0 51.7 %all-reduce.2.cloned.1.call-start = ((), (), s32[]{:S(2)}) async-start(), calls=%async_computation.4 | async-start | bytes 262144 | tf_op jit(solution)/shard_map/psum | solution.py:62
Sparse Core Ops, SparseCore 0:
  75.1 19.5 reduce-scatter.1
  97.0 29.6 all-reduce.1
where the time goes:
time: 136 us; the launch traced here: 135 us
  waiting for transfers between devices  55.2 us (41%)
  local copies, waits for them, and re-layouts  18.6 us (14%)
  blocking collectives  17.8 us (13%)
  between operations  13.5 us (10%)
  starting transfers between devices  13.1 us (10%)
  other arithmetic  10.2 us (7%)
  matrix products  6.73 us (5%)
    psum x1, waiting for transfers between devices, per_device(): gradient = lax.psum(summed, ('tm', 'coef'))  32 us
    reduce_scatter x1, waiting for transfers between devices, per_device(): lax.psum_scatter(partial_grad, 'track', scatter_dimension=0, tiled=True)  19.6 us
    all_gather x1, blocking collectives, per_device(): every_block = lax.all_gather(rounded, 'track', axis=0, tiled=True)  14.5 us
    all_to_all x1, starting transfers between devices, per_device(): lax.all_to_all(labels, ('track', 'tm'), split_axis=0, concat_axis=0, tile...  7.25 us
    all_to_all x1, starting transfers between devices, per_device(): lax.all_to_all(outgoing, ('track', 'tm'), split_axis=0, concat_axis=0, ti...  5.72 us
    scatter x1, local copies, waits for them, and re-layouts, per_device(): jnp.zeros((6, sector_total * slot_count + 1), jnp.float32).at[:, target]  4.45 us
    scatter x1, local copies, waits for them, and re-layouts, per_device(): jnp.zeros((6, owners * capacity), jnp.float32).at[:, placing].set(payload)  4.36 us
    another operation x4, other arithmetic  4.31 us
  transfers between devices with their start and end apart: 4, of which 3 were waited for; matrix products, arithmetic and copies ran while one was open for 13% of the time, Pallas kernels for 0%

commit v1 on v0

--- a/solution.py
+++ b/solution.py
@@ -15,7 +15,13 @@
     row_total = sector_ids.shape[0]
     capacity = 2 * row_total // owners
     rounded = coefficients.astype(jnp.bfloat16)
-    every_block = lax.all_gather(rounded, "track", axis=0, tiled=True)
+    size = lax.axis_size("track")
+    held, pieces = (rounded, [rounded])
+    for _ in range(size - 1):
+        held = lax.ppermute(held, "track", [(i, (i + 1) % size) for i in range(size)])
+        pieces.insert(0, held)
+    line = jnp.concatenate(pieces, axis=0)
+    every_block = jnp.roll(line, (lax.axis_index("track") + 1) * rounded.shape[0], axis=0)
     owner_of = sector_ids // sector_total
     local_sector = sector_ids % sector_total
     onehot = (owner_of[:, None] == jnp.arange(owners, dtype=jnp.int32)[None, :]).astype(jnp.int32)

time: 136 us -> 129 us (0.949)
  blocking collectives: 17.8 us -> 3.3 us
  waiting for transfers between devices: 55.2 us -> 59.6 us
  starting transfers between devices: 13.1 us -> 16.1 us
    all_gather x1 -> x0, blocking collectives: 14.5 us -> none  [per_device(): every_block = lax.all_gather(rounded, 'track', axis=0, tiled=True)]
    ppermute x0 -> x3, starting transfers between devices: none -> 5.22 us  [per_device(): lax.ppermute(held, 'track', [(i, (i + 1) % size) for i in range(size)])]
    ppermute x0 -> x3, waiting for transfers between devices: none -> 4.8 us  [per_device(): lax.ppermute(held, 'track', [(i, (i + 1) % size) for i in range(size)])]
    all_to_all x1, waiting for transfers between devices: 3.54 us -> 0.01 us  [per_device(): lax.all_to_all(outgoing, ('track', 'tm'), split_axis=0, concat_axis=0, ti...]
    reduce_scatter x1, waiting for transfers between devices: 19.6 us -> 22.8 us  [per_device(): lax.psum_scatter(partial_grad, 'track', scatter_dimension=0, tiled=True)]
    all_to_all x1, starting transfers between devices: 7.25 us -> 4.79 us  [per_device(): lax.all_to_all(labels, ('track', 'tm'), split_axis=0, concat_axis=0, tile...]
  transfers between devices with their start and end apart: 4 -> 7, of which waited for: 3 -> 4; matrix products, arithmetic and copies ran while one was open for 13% -> 18% of each run, Pallas kernels for 0% -> 0%
where the time goes in v1:
time: 129 us; the launch traced here: 128 us
  waiting for transfers between devices  59.6 us (46%)
  local copies, waits for them, and re-layouts  18.7 us (14%)
  starting transfers between devices  16.1 us (12%)
  between operations  13.6 us (11%)
  other arithmetic  10.3 us (8%)
  matrix products  6.73 us (5%)
  blocking collectives  3.3 us (3%)
    psum x1, waiting for transfers between devices, per_device(): gradient = lax.psum(summed, ('tm', 'coef'))  31.9 us
    reduce_scatter x1, waiting for transfers between devices, per_device(): lax.psum_scatter(partial_grad, 'track', scatter_dimension=0, tiled=True)  22.8 us
    all_to_all x1, starting transfers between devices, per_device(): lax.all_to_all(outgoing, ('track', 'tm'), split_axis=0, concat_axis=0, ti...  6 us
    ppermute x3, starting transfers between devices, per_device(): lax.ppermute(held, 'track', [(i, (i + 1) % size) for i in range(size)])  5.22 us
    ppermute x3, waiting for transfers between devices, per_device(): lax.ppermute(held, 'track', [(i, (i + 1) % size) for i in range(size)])  4.8 us
    all_to_all x1, starting transfers between devices, per_device(): lax.all_to_all(labels, ('track', 'tm'), split_axis=0, concat_axis=0, tile...  4.79 us
    scatter x1, local copies, waits for them, and re-layouts, per_device(): jnp.zeros((6, sector_total * slot_count + 1), jnp.float32).at[:, target]  4.45 us
    scatter x1, local copies, waits for them, and re-layouts, per_device(): jnp.zeros((6, owners * capacity), jnp.float32).at[:, placing].set(payload)  4.36 us
  transfers between devices with their start and end apart: 7, of which 4 were waited for; matrix products, arithmetic and copies ran while one was open for 18% of the time, Pallas kernels for 0%

profile of v1, /device:TPU:0, one launch (start us, length us, event | category | flops | bytes accessed | tf_op | source)
XLA Modules:
  0.0 128.3 jit_solution(11754154313145519327)
XLA Ops:
  6.5 0.0 copy-start
  6.5 1.0 convert_element_type.18
  7.5 3.0 %collective-permute-start = (bf16[256,128]{1,0:T(8,128)(2,1)S(1)}, bf16[256,128]{1,0:T(8,128)(2,1)S(1)}, u32[]{:S(2)}, u32[]{:S(2)}) collective-permute-start(bf16[256,128]{1,0:T(8,128)(2,1)S(1)} %convert_element_type.18), channel_id=1, source_target_pairs={{0,4},{4,8},{8,12},{12,0},{1,5},{5,9},{9,13},{13,1},{2,6},{6,10},{... | collective-permute-start | bytes 196616 | tf_op jit(solution)/shard_map/ppermute | solution.py:21
  10.5 0.7 add_select_fusion
  11.2 1.7 %reduce-window.14 = s32[8,6,128]{2,0,1:T(8,128)S(1)} reduce-window(s32[8,6,128]{2,0,1:T(8,128)S(1)} %fusion.13, s32[]{:T(128)} %constant.93.clone.1), window={size=1x1x128 pad=0_0x0_0x127_0}, to_apply=%region_0.1 | reduce-window | flops 780288 | bytes 49156 | tf_op jit(solution)/shard_map/reduce-window
  13.0 0.1 slice.30
  13.0 0.1 copy.24
  13.2 0.2 reduce-window.15
  13.3 0.1 copy.25
  13.4 0.1 fusion.11
  13.5 3.4 %scatter_custom_fusion = s32[1536]{0:T(1024)S(1)} fusion(s32[768]{0:T(1024)S(1)} %compare_select_fusion.2, s32[768]{0:T(1024)S(1)} %get-tuple-element.7, s32[]{:T(128)} %constant.97.clone.1), kind=kCustom, calls=%fused_computation.58 | custom fusion | bytes 6148 | tf_op jit(solution)/shard_map/scatter | solution.py:33
  16.9 0.7 all_to_all.9
  17.6 4.8 %all-to-all-start = ((s32[8,1,192]{2,1,0:T(1,128)}), s32[8,1,192]{2,1,0:T(1,128)S(1)}, u32[]{:S(2)}, u32[]{:S(2)}) async-start(s32[8,1,192]{2,1,0:T(1,128)} %all_to_all.9), calls=%async_computation | async-start | bytes 16384 | tf_op jit(solution)/shard_map/all_to_all | solution.py:37
  22.4 0.7 compare_select_fusion.1
  23.1 0.8 reshape.166
  23.8 0.1 reshape.175
  23.9 0.8 compare_and_fusion
  24.7 0.7 maximum_bitcast_fusion
  25.5 0.2 copy.26
  25.7 4.4 %scatter_custom_fusion.1 = f32[6,1536]{0,1:T(8,128)S(1)} fusion(s32[768]{0:T(1024)S(1)} %compare_select_fusion.2, f32[768,6]{1,0:T(8,128)S(1)} %copy.26, f32[]{:T(128)} %constant.92.clone.1), kind=kCustom, calls=%fused_computation.7 | custom fusion | bytes 36868 | tf_op jit(solution)/shard_map/scatter | solution.py:31
  30.0 1.0 copy.27
  31.0 0.0 all-to-all-done
  31.0 6.0 %all-to-all-start.1 = ((f32[8,6,192]{2,1,0:T(8,128)}), f32[8,6,192]{2,1,0:T(8,128)S(1)}, u32[]{:S(2)}, u32[]{:S(2)}) async-start(f32[8,6,192]{2,1,0:T(8,128)} %bitcast.8), calls=%async_computation.1 | async-start | bytes 131072 | tf_op jit(solution)/shard_map/all_to_all | solution.py:36
  37.0 0.0 reduce-scatter.2.cloned.1.call-start
  37.1 0.1 eq.64
  37.2 0.1 eq.60
  37.2 2.3 %reduce-window.16 = s32[8,12,128]{2,1,0:T(8,128)S(1)} reduce-window(s32[8,12,128]{2,1,0:T(8,128)S(1)} %fusion.8, s32[]{:T(128)} %constant.93.clone.1), window={size=1x1x128 pad=0_0x0_0x127_0}, to_apply=%region_4.5 | reduce-window | flops 1560576 | bytes 98308 | tf_op jit(solution)/shard_map/reduce-window.2
  39.5 0.3 slice_reduce_fusion
  39.8 0.2 reduce-window.19
  40.0 0.1 add_bitcast_fusion
  40.1 0.1 mul.46
  40.2 0.1 ge.21
  40.3 0.0 collective-permute-done
  40.3 2.0 %collective-permute-start.1 = (bf16[256,128]{1,0:T(8,128)(2,1)S(1)}, bf16[256,128]{1,0:T(8,128)(2,1)S(1)}, u32[]{:S(2)}, u32[]{:S(2)}) collective-permute-start(bf16[256,128]{1,0:T(8,128)(2,1)S(1)} %collective-permute-done), channel_id=1, source_target_pairs={{0,4},{4,8},{8,12},{12,0},{1,5},{5,9},{9,13},{13,1},{2,6},{6,10},{... | collective-permute-start | bytes 196616 | tf_op jit(solution)/shard_map/ppermute | solution.py:21
  42.3 4.1 %collective-permute-done.1 = bf16[256,128]{1,0:T(8,128)(2,1)S(1)} collective-permute-done((bf16[256,128]{1,0:T(8,128)(2,1)S(1)}, bf16[256,128]{1,0:T(8,128)(2,1)S(1)}, u32[]{:S(2)}, u32[]{:S(2)}) %collective-permute-start.1) | collective-permute-done | bytes 65568 | tf_op jit(solution)/shard_map/ppermute | solution.py:21
  46.4 0.2 collective-permute-start.2
  46.6 0.0 all-to-all-done.1
  46.6 0.1 reshape.198
  46.7 0.3 copy.29
  47.0 4.4 %scatter_custom_fusion.2 = f32[6,1025]{0,1:T(8,128)S(1)} fusion(s32[1536]{0:T(1024)S(1)} %fusion.17, f32[1536,6]{1,0:T(8,128)S(1)} %copy.29, f32[]{:T(128)} %constant.92.clone.1), kind=kCustom, calls=%fused_computation.9 | custom fusion | bytes 24604 | tf_op jit(solution)/shard_map/scatter | solution.py:48
  51.5 0.2 copy.36
  51.7 0.7 collective-permute-done.2
  52.5 0.0 copy-done
  52.6 0.6 gather_fusion
  53.3 0.1 select_bitcast_fusion
  53.4 3.7 %fusion = f32[8,1,3,128,1]{3,1,4,2,0:T(1,128)S(1)} fusion(bf16[8,6,3,128,128]{4,3,2,1,0:T(8,128)(2,1)} %param.13, bf16[8,6,128,1,1]{2,1,0,3,4:T(8,128)(2,1)S(1)} %select_bitcast_fusion), kind=kOutput, calls=%fused_computation.5 | convolution fusion | flops 4718592 | bytes 4743168 | tf_op jit(solution)/shard_map/skcjb,skb->scj/dot_general | solution.py:56
  57.0 3.3 %psum.14 = f32[8,3,128]{2,0,1:T(8,128)S(1)} all-reduce(f32[8,3,128]{2,0,1:T(8,128)S(1)} %bitcast.50), channel_id=1, replica_groups=mesh['parts'=2,'track'=4,'tm'=2,'coef'=2] {'coef'}, use_global_device_ids=true, to_apply=%region_9.10 | all-reduce | flops 3072 | bytes 24576 | tf_op jit(solution)/shard_map/psum | solution.py:59
  60.3 3.1 %fusion.15 = f32[8,1,6,128,1]{3,1,4,2,0:T(1,128)S(1)} fusion(bf16[8,6,3,128,128]{4,3,2,1,0:T(8,128)(2,1)} %param.13, bf16[8,3,128,1,1]{2,0,1,3,4:T(8,128)(2,1)S(1)} %fusion.18), kind=kOutput, calls=%fused_computation.42 | convolution fusion | flops 4718592 | bytes 4749312 | tf_op jit(solution)/shard_map/skcjb,scj->skb/dot_general | solution.py:62
  63.4 0.1 bitcast_select_fusion
  63.5 1.5 %scatter_custom_fusion.3 = f32[1024,128]{1,0:T(8,128)} fusion(s32[48]{0:T(128)S(1)} %fusion.23, f32[48,128]{1,0:T(8,128)S(1)} %reshape.209, f32[]{:T(128)} %constant.92.clone.1), kind=kCustom, calls=%fused_computation.11 | custom fusion | flops 6144 | bytes 524292 | tf_op jit(solution)/shard_map/scatter-add | solution.py:66
  65.0 0.0 reduce-scatter.2.cloned.1.call-update
  65.1 0.0 all-reduce.2.cloned.1.call-start
  65.1 22.8 %reduce-scatter.2.cloned.1.call-done = f32[256,128]{1,0:T(8,128)} async-done(((f32[1024,128]{1,0:T(8,128)}), f32[256,128]{1,0:T(8,128)}) %reduce-scatter.2.cloned.1.call-update) | async-done | bytes 131088 | tf_op jit(solution)/shard_map/reduce_scatter | solution.py:67
  87.9 0.0 all-reduce.2.cloned.1.call-update
  88.0 31.9 %all-reduce.2.cloned.1.call-done = f32[256,128]{1,0:T(8,128)} async-done(((f32[256,128]{1,0:T(8,128)}), f32[256,128]{1,0:T(8,128)}) %all-reduce.2.cloned.1.call-update) | async-done | bytes 131088 | tf_op jit(solution)/shard_map/psum | solution.py:68
  119.9 1.6 %copy.56 = f32[256,128]{1,0:T(8,128)} copy(f32[256,128]{1,0:T(8,128)} %all-reduce.2.cloned.1.call-done) | data formatting | bytes 262144
  (25 shorter events, 0.4 us)
Async XLA Ops:
  6.5 46.0 %copy-start = (f32[256,128]{1,0:T(8,128)S(1)}, f32[256,128]{1,0:T(8,128)}, u32[]{:S(2)}) copy-start(f32[256,128]{1,0:T(8,128)} %param.10) | copy-start | bytes 393220
  7.5 32.8 %collective-permute-start = (bf16[256,128]{1,0:T(8,128)(2,1)S(1)}, bf16[256,128]{1,0:T(8,128)(2,1)S(1)}, u32[]{:S(2)}, u32[]{:S(2)}) collective-permute-start(bf16[256,128]{1,0:T(8,128)(2,1)S(1)} %convert_element_type.18), channel_id=1, source_target_pairs={{0,4},{4,8},{8,12},{12,0},{1,5},{5,9},{9,13},{13,1},{2,6},{6,10},{... | collective-permute-start | bytes 196616 | tf_op jit(solution)/shard_map/ppermute | solution.py:21
  17.6 13.4 %all-to-all-start = ((s32[8,1,192]{2,1,0:T(1,128)}), s32[8,1,192]{2,1,0:T(1,128)S(1)}, u32[]{:S(2)}, u32[]{:S(2)}) async-start(s32[8,1,192]{2,1,0:T(1,128)} %all_to_all.9), calls=%async_computation | async-start | bytes 16384 | tf_op jit(solution)/shard_map/all_to_all | solution.py:37
  31.0 15.6 %all-to-all-start.1 = ((f32[8,6,192]{2,1,0:T(8,128)}), f32[8,6,192]{2,1,0:T(8,128)S(1)}, u32[]{:S(2)}, u32[]{:S(2)}) async-start(f32[8,6,192]{2,1,0:T(8,128)} %bitcast.8), calls=%async_computation.1 | async-start | bytes 131072 | tf_op jit(solution)/shard_map/all_to_all | solution.py:36
  37.0 50.9 %reduce-scatter.2.cloned.1.call-start = ((), (), s32[]{:S(2)}) async-start(), calls=%async_computation.3 | async-start | bytes 655360 | tf_op jit(solution)/shard_map/reduce_scatter | solution.py:67
  40.3 6.1 %collective-permute-start.1 = (bf16[256,128]{1,0:T(8,128)(2,1)S(1)}, bf16[256,128]{1,0:T(8,128)(2,1)S(1)}, u32[]{:S(2)}, u32[]{:S(2)}) collective-permute-start(bf16[256,128]{1,0:T(8,128)(2,1)S(1)} %collective-permute-done), channel_id=1, source_target_pairs={{0,4},{4,8},{8,12},{12,0},{1,5},{5,9},{9,13},{13,1},{2,6},{6,10},{... | collective-permute-start | bytes 196616 | tf_op jit(solution)/shard_map/ppermute | solution.py:21
  46.4 6.1 %collective-permute-start.2 = (bf16[256,128]{1,0:T(8,128)(2,1)S(1)}, bf16[256,128]{1,0:T(8,128)(2,1)S(1)}, u32[]{:S(2)}, u32[]{:S(2)}) collective-permute-start(bf16[256,128]{1,0:T(8,128)(2,1)S(1)} %collective-permute-done.1), channel_id=1, source_target_pairs={{0,4},{4,8},{8,12},{12,0},{1,5},{5,9},{9,13},{13,1},{2,6},{6,10},{... | collective-permute-start | bytes 196616 | tf_op jit(solution)/shard_map/ppermute | solution.py:21
  65.1 54.8 %all-reduce.2.cloned.1.call-start = ((), (), s32[]{:S(2)}) async-start(), calls=%async_computation.4 | async-start | bytes 262144 | tf_op jit(solution)/shard_map/psum | solution.py:68
Sparse Core Ops, SparseCore 0:
  65.2 22.7 reduce-scatter.1
  90.2 29.6 all-reduce.1
